TPU v7x, 768 devices: a whole 4x8x12 slice. The times are simulated.
768 devices in a mesh: gx: 96 (over y_hi, z, core), yz: 8 (over y_lo, x).
Axes of the slice: x: 4, y: 8 (y_hi: 4, y_lo: 2; y = y_hi * 2 + y_lo), z: 12, core: 2. Of those that a mesh axis runs over, the one named last changes fastest.
Arguments:
- right_side: float32 [384, 256, 512], P('gx', 'yz'), may hold values from -36 to 36
- potential: float32 [384, 256, 512], P('gx', 'yz'), may hold values from -3 to 3
- permittivity: float32 [384, 256, 512], P('gx', 'yz'), may hold values from 0.1 to 4
- ion_mask: int32 [384, 256, 512], P('gx', 'yz'), may hold values 0 or 1
Outputs:
- solution_field: float32 [384, 256, 512], P('gx', 'yz')
- residual: float32 [384, 256, 512], P('gx', 'yz')
All inputs are finite; a program needn't handle non-finite values. No bound on the sum of `ion_mask` on one device may be relied on, other than what follows from the above.
Results may differ from a plain program's by a relative error of at most 0.03.
Values sent between devices are 32-bit elements; how exact they have to be, the bound alone decides.
A program may use at most 32 MiB of HBM per device.

v0:
```python
import jax
import jax.numpy as jnp
from jax import lax
from jax.sharding import PartitionSpec as P


def extended(cells, sides, width):
    for axis, dim in sides:
        count = lax.axis_size(axis)
        ends = count - 1
        head = lax.slice_in_dim(cells, 0, width, axis=dim)
        tail = lax.slice_in_dim(cells, cells.shape[dim] - width, cells.shape[dim], axis=dim)
        cells = jnp.concatenate(
            [
                lax.ppermute(tail, axis, [(i, (i + 1) % count) for i in range(ends)]),
                cells,
                lax.ppermute(head, axis, [((i + 1) % count, i) for i in range(ends)]),
            ],
            axis=dim,
        )
    return cells


def six_sides(padded):
    return [
        padded[2:, 1:-1, 1:-1],
        padded[:-2, 1:-1, 1:-1],
        padded[1:-1, 2:, 1:-1],
        padded[1:-1, :-2, 1:-1],
        padded[1:-1, 1:-1, 2:],
        padded[1:-1, 1:-1, :-2],
    ]


def preconditioned(residual_now, scaled_now):
    return lax.psum(jnp.sum(residual_now * scaled_now), ("gx", "yz"))


def local(right_side, potential, permittivity, ion_mask):
    rim = extended(permittivity, (("gx", 0), ("yz", 1)), 1)
    sides = six_sides(jnp.pad(rim, ((0, 0), (0, 0), (1, 1))))
    faces = [
        jnp.where(other > 0, 2.0 * permittivity * other / (permittivity + other), permittivity)
        for other in sides
    ]
    ionic = 0.5 * ion_mask.astype(jnp.float32) * jnp.cosh(potential)
    diag = ionic + faces[0] + faces[1] + faces[2] + faces[3] + faces[4] + faces[5]
    solution_field = jnp.zeros_like(right_side)
    residual = right_side
    scaled = residual / diag
    direction = scaled
    rz_now = preconditioned(residual, scaled)
    for step in range(2):
        padded = extended(direction, (("gx", 0), ("yz", 1)), 1)
        near = six_sides(jnp.pad(padded, ((0, 0), (0, 0), (1, 1))))
        total = diag * direction
        for face, operate_other in zip(faces, near):
            total = total - face * operate_other
        alpha = rz_now / lax.psum(jnp.sum(direction * total), ("gx", "yz"))
        solution_field = solution_field + alpha * direction
        residual = residual - alpha * total
        if step < 1:
            scaled = residual / diag
            rz_next = preconditioned(residual, scaled)
            direction = scaled + rz_next / rz_now * direction
            rz_now = rz_next
    return (solution_field, residual)


def solution(mesh):
    in_specs = (P("gx", "yz", None), P("gx", "yz", None), P("gx", "yz", None), P("gx", "yz", None))
    out_specs = (P("gx", "yz", None), P("gx", "yz", None))
    return jax.shard_map(local, mesh=mesh, in_specs=in_specs, out_specs=out_specs, check_vma=False)
```

profile of v0, /device:TPU:1, one launch (start us, length us, event | category | flops | bytes accessed | tf_op | source)
XLA Modules:
  0.0 403.0 jit_solution(2434433401207880028)
XLA Ops:
  0.6 0.9 fusion.29
  1.6 5.4 %collective-permute-start.1 = (f32[1,32,512]{2,1,0:T(8,128)S(1)}, f32[1,32,512]{2,1,0:T(8,128)S(1)}, u32[]{:S(2)}, u32[]{:S(2)}) collective-permute-start(f32[1,32,512]{2,1,0:T(8,128)S(1)} %get-tuple-element.27), channel_id=1, source_target_pairs={{0,8},{8,16},{16,24},{24,32},{32,40},{40,48},{48,56},{56,64},{64,7... | collective-permute-start | bytes 196616 | tf_op jit(solution)/shard_map/ppermute | solution.py:15
  7.0 8.3 %collective-permute-start = (f32[1,32,512]{2,1,0:T(8,128)S(1)}, f32[1,32,512]{2,1,0:T(8,128)S(1)}, u32[]{:S(2)}, u32[]{:S(2)}) collective-permute-start(f32[1,32,512]{2,1,0:T(8,128)S(1)} %get-tuple-element.26), channel_id=1, source_target_pairs={{8,0},{16,8},{24,16},{32,24},{40,32},{48,40},{56,48},{64,56},{72,6... | collective-permute-start | bytes 196616 | tf_op jit(solution)/shard_map/ppermute | solution.py:17
  15.4 0.8 collective-permute-done
  16.2 1.3 collective-permute-start.3
  17.5 0.0 copy-start.1
  17.5 0.0 copy-start.2
  17.5 1.4 collective-permute-start.2
  19.0 3.1 collective-permute-done.2
  22.1 0.3 select_maximum_fusion.8
  22.5 0.6 fusion.25
  23.0 1.9 collective-permute-start.5
  25.0 2.8 collective-permute-start.4
  27.8 2.8 collective-permute-done.4
  30.6 2.7 collective-permute-start.7
  33.3 1.3 collective-permute-start.6
  34.6 3.1 collective-permute-done.6
  37.7 0.3 select_maximum_fusion.4
  38.0 1.2 multiply_reduce_fusion.2
  39.2 122.9 %all-reduce.3 = (f32[]{:T(128)}, f32[]{:T(128)}) all-reduce(f32[]{:T(128)} %get-tuple-element.3, f32[]{:T(128)} %get-tuple-element.2), channel_id=1, replica_groups=mesh['gx'=96,'yz'=8] {'gx','yz'}, use_global_device_ids=true, to_apply=%region_1.2 | all-reduce | flops 2 | bytes 16 | tf_op jit(solution)/shard_map/psum | solution.py:36
  163.5 0.7 multiply_reduce_fusion.1
  164.2 103.7 %psum.30 = f32[]{:T(128)} all-reduce(f32[]{:T(128)} %get-tuple-element.8), channel_id=1, replica_groups=mesh['gx'=96,'yz'=8] {'gx','yz'}, use_global_device_ids=true, to_apply=%region_5.6 | all-reduce | flops 1 | bytes 8 | tf_op jit(solution)/shard_map/psum | solution.py:36
  269.3 4.2 %collective-permute-start.9 = (f32[1,32,512]{2,1,0:T(8,128)S(1)}, f32[1,32,512]{2,1,0:T(8,128)S(1)}, u32[]{:S(2)}, u32[]{:S(2)}) collective-permute-start(f32[1,32,512]{2,1,0:T(8,128)S(1)} %get-tuple-element.22), channel_id=1, source_target_pairs={{0,8},{8,16},{16,24},{24,32},{32,40},{40,48},{48,56},{56,64},{64,7... | collective-permute-start | bytes 196616 | tf_op jit(solution)/shard_map/ppermute | solution.py:15
  273.5 1.9 collective-permute-start.8
  275.4 3.6 collective-permute-done.8
  279.1 3.6 collective-permute-start.11
  282.8 1.3 collective-permute-start.10
  284.1 3.1 collective-permute-done.10
  287.2 0.3 select_maximum_fusion
  287.5 1.2 multiply_reduce_fusion
  288.7 112.1 %psum.31 = f32[]{:T(128)} all-reduce(f32[]{:T(128)} %get-tuple-element.6), channel_id=1, replica_groups=mesh['gx'=96,'yz'=8] {'gx','yz'}, use_global_device_ids=true, to_apply=%region_7.8 | all-reduce | flops 1 | bytes 8 | tf_op jit(solution)/shard_map/psum | solution.py:59
  402.1 0.9 multiply_subtract_fusion
  (21 shorter events, 0.2 us)
Async XLA Ops:
  0.6 14.7 %copy-start = (f32[4,32,512]{2,1,0:T(8,128)S(1)}, f32[4,32,512]{2,1,0:T(8,128)}, u32[]{:S(2)}) copy-start(f32[4,32,512]{2,1,0:T(8,128)} %param.6) | copy-start | bytes 786436
  1.6 13.7 %collective-permute-start.1 = (f32[1,32,512]{2,1,0:T(8,128)S(1)}, f32[1,32,512]{2,1,0:T(8,128)S(1)}, u32[]{:S(2)}, u32[]{:S(2)}) collective-permute-start(f32[1,32,512]{2,1,0:T(8,128)S(1)} %get-tuple-element.27), channel_id=1, source_target_pairs={{0,8},{8,16},{16,24},{24,32},{32,40},{40,48},{48,56},{56,64},{64,7... | collective-permute-start | bytes 196616 | tf_op jit(solution)/shard_map/ppermute | solution.py:15
  7.0 9.2 %collective-permute-start = (f32[1,32,512]{2,1,0:T(8,128)S(1)}, f32[1,32,512]{2,1,0:T(8,128)S(1)}, u32[]{:S(2)}, u32[]{:S(2)}) collective-permute-start(f32[1,32,512]{2,1,0:T(8,128)S(1)} %get-tuple-element.26), channel_id=1, source_target_pairs={{8,0},{16,8},{24,16},{32,24},{40,32},{48,40},{56,48},{64,56},{72,6... | collective-permute-start | bytes 196616 | tf_op jit(solution)/shard_map/ppermute | solution.py:17
  16.2 2.8 collective-permute-start.3
  17.5 4.9 %copy-start.1 = (f32[4,32,512]{2,1,0:T(8,128)S(1)}, f32[4,32,512]{2,1,0:T(8,128)}, u32[]{:S(2)}) copy-start(f32[4,32,512]{2,1,0:T(8,128)} %param.4) | copy-start | bytes 786436
  17.5 4.9 %copy-start.2 = (f32[4,32,512]{2,1,0:T(8,128)S(1)}, f32[4,32,512]{2,1,0:T(8,128)}, u32[]{:S(2)}) copy-start(f32[4,32,512]{2,1,0:T(8,128)} %param.5) | copy-start | bytes 786436
  17.5 4.9 %copy-start.3 = (s32[4,32,512]{2,1,0:T(8,128)S(1)}, s32[4,32,512]{2,1,0:T(8,128)}, u32[]{:S(2)}) copy-start(s32[4,32,512]{2,1,0:T(8,128)} %param.7) | copy-start | bytes 786436
  17.5 4.6 %collective-permute-start.2 = (f32[6,1,512]{2,1,0:T(1,128)S(1)}, f32[6,1,512]{2,1,0:T(1,128)S(1)}, u32[]{:S(2)}, u32[]{:S(2)}) collective-permute-start(f32[6,1,512]{2,1,0:T(1,128)S(1)} %get-tuple-element.21), channel_id=1, source_target_pairs={{1,0},{2,1},{3,2},{4,3},{5,4},{6,5},{7,6},{9,8},{10,9},{11,10},{12... | collective-permute-start | bytes 36872 | tf_op jit(solution)/shard_map/ppermute | solution.py:17
  23.0 4.7 %collective-permute-start.5 = (f32[1,32,512]{2,1,0:T(8,128)S(1)}, f32[1,32,512]{2,1,0:T(8,128)S(1)}, u32[]{:S(2)}, u32[]{:S(2)}) collective-permute-start(f32[1,32,512]{2,1,0:T(8,128)S(1)} %get-tuple-element.24), channel_id=1, source_target_pairs={{0,8},{8,16},{16,24},{24,32},{32,40},{40,48},{48,56},{56,64},{64,7... | collective-permute-start | bytes 196616 | tf_op jit(solution)/shard_map/ppermute | solution.py:15
  25.0 5.6 %collective-permute-start.4 = (f32[1,32,512]{2,1,0:T(8,128)S(1)}, f32[1,32,512]{2,1,0:T(8,128)S(1)}, u32[]{:S(2)}, u32[]{:S(2)}) collective-permute-start(f32[1,32,512]{2,1,0:T(8,128)S(1)} %get-tuple-element.25), channel_id=1, source_target_pairs={{8,0},{16,8},{24,16},{32,24},{40,32},{48,40},{56,48},{64,56},{72,6... | collective-permute-start | bytes 196616 | tf_op jit(solution)/shard_map/ppermute | solution.py:17
  30.6 4.0 collective-permute-start.7
  33.3 4.4 %collective-permute-start.6 = (f32[6,1,512]{2,1,0:T(1,128)S(1)}, f32[6,1,512]{2,1,0:T(1,128)S(1)}, u32[]{:S(2)}, u32[]{:S(2)}) collective-permute-start(f32[6,1,512]{2,1,0:T(1,128)S(1)} %get-tuple-element.19), channel_id=1, source_target_pairs={{1,0},{2,1},{3,2},{4,3},{5,4},{6,5},{7,6},{9,8},{10,9},{11,10},{12... | collective-permute-start | bytes 36872 | tf_op jit(solution)/shard_map/ppermute | solution.py:17
  269.3 6.2 %collective-permute-start.9 = (f32[1,32,512]{2,1,0:T(8,128)S(1)}, f32[1,32,512]{2,1,0:T(8,128)S(1)}, u32[]{:S(2)}, u32[]{:S(2)}) collective-permute-start(f32[1,32,512]{2,1,0:T(8,128)S(1)} %get-tuple-element.22), channel_id=1, source_target_pairs={{0,8},{8,16},{16,24},{24,32},{32,40},{40,48},{48,56},{56,64},{64,7... | collective-permute-start | bytes 196616 | tf_op jit(solution)/shard_map/ppermute | solution.py:15
  273.5 5.6 %collective-permute-start.8 = (f32[1,32,512]{2,1,0:T(8,128)S(1)}, f32[1,32,512]{2,1,0:T(8,128)S(1)}, u32[]{:S(2)}, u32[]{:S(2)}) collective-permute-start(f32[1,32,512]{2,1,0:T(8,128)S(1)} %get-tuple-element.23), channel_id=1, source_target_pairs={{8,0},{16,8},{24,16},{32,24},{40,32},{48,40},{56,48},{64,56},{72,6... | collective-permute-start | bytes 196616 | tf_op jit(solution)/shard_map/ppermute | solution.py:17
  279.1 5.0 %collective-permute-start.11 = (f32[6,1,512]{2,1,0:T(1,128)S(1)}, f32[6,1,512]{2,1,0:T(1,128)S(1)}, u32[]{:S(2)}, u32[]{:S(2)}) collective-permute-start(f32[6,1,512]{2,1,0:T(1,128)S(1)} %get-tuple-element.16), channel_id=1, source_target_pairs={{0,1},{1,2},{2,3},{3,4},{4,5},{5,6},{6,7},{8,9},{9,10},{10,11},{11... | collective-permute-start | bytes 36872 | tf_op jit(solution)/shard_map/ppermute | solution.py:15
  282.8 4.4 %collective-permute-start.10 = (f32[6,1,512]{2,1,0:T(1,128)S(1)}, f32[6,1,512]{2,1,0:T(1,128)S(1)}, u32[]{:S(2)}, u32[]{:S(2)}) collective-permute-start(f32[6,1,512]{2,1,0:T(1,128)S(1)} %get-tuple-element.17), channel_id=1, source_target_pairs={{1,0},{2,1},{3,2},{4,3},{5,4},{6,5},{7,6},{9,8},{10,9},{11,10},{12... | collective-permute-start | bytes 36872 | tf_op jit(solution)/shard_map/ppermute | solution.py:17
where the time goes:
time: 404 us; the launch traced here: 403 us
  blocking collectives  339 us (84%)
  starting transfers between devices  36.2 us (9%)
  waiting for transfers between devices  16.6 us (4%)
  other arithmetic  5.51 us (1%)
  between operations  4.92 us (1%)
    psum x2, blocking collectives, preconditioned(): return lax.psum(jnp.sum(residual_now * scaled_now), ('gx', 'yz'))  227 us
    psum x1, blocking collectives, local(): alpha = rz_now / lax.psum(jnp.sum(direction * total), ('gx', 'yz'))  112 us
    ppermute x6, starting transfers between devices, extended(): lax.ppermute(tail, axis, [(i, (i + 1) % count) for i in range(ends)])  19.2 us
    ppermute x6, starting transfers between devices, extended(): lax.ppermute(head, axis, [((i + 1) % count, i) for i in range(ends)])  17 us
    ppermute x6, waiting for transfers between devices, extended(): lax.ppermute(head, axis, [((i + 1) % count, i) for i in range(ends)])  16.6 us
  transfers between devices with their start and end apart: 12, of which 6 were waited for; matrix products, arithmetic and copies ran while one was open for 0% of the time, Pallas kernels for 0%

commit v1 on v0

v1 whole, which is shorter than its diff:
```python
import functools

import jax
import jax.numpy as jnp
from jax import lax
from jax.experimental import pallas as pl
from jax.experimental.pallas import tpu as pltpu
from jax.sharding import PartitionSpec as P

MESH = pl.DeviceIdType.MESH
SIZES = dict(y_hi=4, z=12, core=2, y_lo=2, x=4)


def face(a, b):
    return (2.0 * a * b) / (a + b)


def kernel(sizes, b_hbm, p_hbm, e_hbm, m_hbm, x_out, r_out,
           B, PT, E, M, CX, CXE, CY, CYE, CZ, D, RD, Z, Q, U, W, XO, RO,
           XR, YR, YS, part, sums, g0, g1, g2,
           in_sem, out_sem, hs_sem, hr_sem, as_sem, ar_sem):
    nyh, nz, nc, nyl, nx = (sizes[k] for k in ("y_hi", "z", "core", "y_lo", "x"))
    ngx, nyz = nyh * nz * nc, nyl * nx
    gx, yz = lax.axis_index("gx"), lax.axis_index("yz")
    core, zz, yh = gx % nc, (gx // nc) % nz, gx // (nc * nz)
    xx, yl = yz % nx, yz // nx
    ny = nyh * nyl
    yy = yh * nyl + yl
    planes, rows, lanes = E.shape
    tiles = rows // 8

    left = ((gx + ngx - 1) % ngx, yz)
    right = ((gx + 1) % ngx, yz)
    down = (gx, (yz + nyz - 1) % nyz)
    up = (gx, (yz + 1) % nyz)
    near = (left, right, down, up)

    def place(yh_, z_, c_, yl_, x_):
        return ((yh_ * nz + z_) * nc + c_, yl_ * nx + x_)

    na = nx * nc
    ia = xx * nc + core
    group_a = [place(yh, zz, ((ia + d) % na) % nc, yl, ((ia + d) % na) // nc) for d in range(1, na)]
    group_b = [place(((yy + d) % ny) // nyl, zz, core, ((yy + d) % ny) % nyl, xx) for d in range(1, ny)]
    group_c = [place(yh, (zz + d) % nz, core, yl, xx) for d in range(1, nz)]
    groups = (group_a, group_b, group_c)

    barrier = pltpu.get_barrier_semaphore()
    count = 0
    for peer in near + tuple(group_a) + tuple(group_b) + tuple(group_c):
        pl.semaphore_signal(barrier, inc=1, device_id=peer, device_id_type=MESH)
        count += 1

    loads = [pltpu.make_async_copy(s, d, in_sem.at[i])
             for i, (s, d) in enumerate(((e_hbm, E), (p_hbm, PT), (m_hbm, M), (b_hbm, B)))]
    for c in loads:
        c.start()

    x_lo, x_hi = gx > 0, gx < ngx - 1
    y_lo, y_hi = yz > 0, yz < nyz - 1
    lane = lax.broadcasted_iota(jnp.int32, (8, lanes), 1)
    sub = lax.broadcasted_iota(jnp.int32, (8, lanes), 0)

    def at(j):
        return slice(8 * j, 8 * j + 8)

    def before(ref, p, j):
        if j == 0:
            return pltpu.roll(ref[p, at(0), :], 1, 0)
        return ref[p, 8 * j - 1:8 * j + 7, :]

    def after(ref, p, j):
        if j == tiles - 1:
            return pltpu.roll(ref[p, at(j), :], 7, 0)
        return ref[p, 8 * j + 1:8 * j + 9, :]

    def exchange(n, field):
        copies = []
        for k, (src, dst, dev) in enumerate((
                (YS.at[n, 0], YR.at[n, 1], down), (YS.at[n, 1], YR.at[n, 0], up),
                (field.at[0], XR.at[n, 1], left), (field.at[planes - 1], XR.at[n, 0], right))):
            c = pltpu.make_async_remote_copy(src_ref=src, dst_ref=dst, send_sem=hs_sem.at[n, k],
                                             recv_sem=hr_sem.at[n, k], device_id=dev, device_id_type=MESH)
            c.start()
            copies.append(c)
        return copies

    loads[0].wait()
    YS[0, 0] = E[:, 0, :]
    YS[0, 1] = E[:, rows - 1, :]
    pl.semaphore_wait(barrier, count)
    sent = exchange(0, E)

    CY[:, rows:rows + 8, :] = jnp.zeros((planes, 8, lanes), jnp.float32)
    for p in range(planes):
        for j in range(tiles):
            e = E[p, at(j), :]
            CZ[p, at(j), :] = jnp.where(lane == lanes - 1, 0.0, face(e, pltpu.roll(e, lanes - 1, 1)))
            cy = face(e, before(E, p, j))
            CY[p, at(j), :] = jnp.where(sub == 0, 0.0, cy) if j == 0 else cy
            if p < planes - 1:
                CX[p, at(j), :] = face(e, E[p + 1, at(j), :])
    loads[1].wait()
    loads[2].wait()
    for p in range(planes):
        for j in range(tiles):
            e, cz = E[p, at(j), :], CZ[p, at(j), :]
            pt = PT[p, at(j), :]
            d = 0.25 * M[p, at(j), :].astype(jnp.float32) * (jnp.exp(pt) + jnp.exp(-pt))
            d = d + cz + pltpu.roll(cz, 1, 1) + jnp.where((lane == 0) | (lane == lanes - 1), e, 0.0)
            d = d + CY[p, at(j), :] + CY[p, 8 * j + 1:8 * j + 9, :]
            if p > 0:
                d = d + CX[p - 1, at(j), :]
            if p < planes - 1:
                d = d + CX[p, at(j), :]
            D[p, at(j), :] = d

    loads[3].wait()
    for c in sent:
        c.wait_recv()
    for k, row, inside in ((0, 0, y_lo), (1, rows - 1, y_hi)):
        e = E[:, row, :]
        n = jnp.where(inside, YR[0, k], 0.0)
        c = face(e, n)
        CYE[k] = c
        D[:, row, :] = D[:, row, :] + jnp.where(inside, c, e)
    for k, p, inside in ((0, 0, x_lo), (1, planes - 1, x_hi)):
        for j in range(tiles):
            e = E[p, at(j), :]
            n = jnp.where(inside, XR[0, k, at(j), :], 0.0)
            c = face(e, n)
            CXE[k, at(j), :] = c
            d = D[p, at(j), :] + jnp.where(inside, c, e)
            rd = 1.0 / d
            D[p, at(j), :] = d
            RD[p, at(j), :] = rd
            Z[p, at(j), :] = B[p, at(j), :] * rd
    for p in range(1, planes - 1):
        for j in range(tiles):
            rd = 1.0 / D[p, at(j), :]
            RD[p, at(j), :] = rd
            Z[p, at(j), :] = B[p, at(j), :] * rd
    YS[1, 0] = Z[:, 0, :]
    YS[1, 1] = Z[:, rows - 1, :]
    sent_z = exchange(1, Z)

    def image(V, p, j):
        v, cz = V[p, at(j), :], CZ[p, at(j), :]
        t = D[p, at(j), :] * v
        t = t - cz * pltpu.roll(v, lanes - 1, 1) - pltpu.roll(cz * v, 1, 1)
        t = t - CY[p, at(j), :] * before(V, p, j) - CY[p, 8 * j + 1:8 * j + 9, :] * after(V, p, j)
        if p > 0:
            t = t - CX[p - 1, at(j), :] * V[p - 1, at(j), :]
        if p < planes - 1:
            t = t - CX[p, at(j), :] * V[p + 1, at(j), :]
        return t

    for p in range(planes):
        for j in range(tiles):
            Q[p, at(j), :] = image(Z, p, j)
    for c in sent_z:
        c.wait_recv()
    for k, row in ((0, 0), (1, rows - 1)):
        Q[:, row, :] = Q[:, row, :] - CYE[k] * YR[1, k]
    for k, p in ((0, 0), (1, planes - 1)):
        for j in range(tiles):
            Q[p, at(j), :] = Q[p, at(j), :] - CXE[k, at(j), :] * XR[1, k, at(j), :]
    s0 = s1 = s2 = s3 = jnp.zeros((8, lanes), jnp.float32)
    for p in range(planes):
        for j in range(tiles):
            U[p, at(j), :] = Q[p, at(j), :] * RD[p, at(j), :]
    YS[2, 0] = U[:, 0, :]
    YS[2, 1] = U[:, rows - 1, :]
    sent_u = exchange(2, U)
    for p in range(planes):
        for j in range(tiles):
            z, q, u = Z[p, at(j), :], Q[p, at(j), :], U[p, at(j), :]
            w = image(U, p, j)
            W[p, at(j), :] = w
            s0 = s0 + B[p, at(j), :] * z
            s1 = s1 + z * q
            s2 = s2 + q * u
            s3 = s3 + u * w
    for c in sent_u:
        c.wait_recv()
    edge = jnp.zeros((planes, lanes), jnp.float32)
    for k, row in ((0, 0), (1, rows - 1)):
        t = CYE[k] * YR[2, k]
        edge = edge + U[:, row, :] * t
        W[:, row, :] = W[:, row, :] - t
    for k, p in ((0, 0), (1, planes - 1)):
        for j in range(tiles):
            t = CXE[k, at(j), :] * XR[2, k, at(j), :]
            s3 = s3 - U[p, at(j), :] * t
            W[p, at(j), :] = W[p, at(j), :] - t

    def folded(s):
        t = s[:, :128]
        for i in range(128, lanes, 128):
            t = t + s[:, i:i + 128]
        return jnp.sum(t, axis=0, keepdims=True)

    part[0, 0:1, :] = folded(s0)
    part[0, 1:2, :] = folded(s1)
    part[0, 2:3, :] = folded(s2)
    part[0, 3:4, :] = folded(s3) - folded(edge)
    sends = []
    for n, (peers, got) in enumerate(zip(groups, (g0, g1, g2))):
        size = len(peers)
        for d, peer in enumerate(peers):
            pltpu.make_async_remote_copy(src_ref=part.at[n], dst_ref=got.at[d], send_sem=as_sem.at[n],
                                         recv_sem=ar_sem.at[n], device_id=peer, device_id_type=MESH).start()
        total = part[n]
        if size:
            pltpu.make_async_copy(got, got, ar_sem.at[n]).wait()
            for d in range(size):
                total = total + got[d]
        part[n + 1] = total
    s = jnp.sum(part[3], axis=1, keepdims=True)
    s0, s1, s2, s3 = s[0:1], s[1:2], s[2:3], s[3:4]
    a, g, h = s0 / s1, s2 / s1, s3 / s1
    cu = (a * g - 1.0) / (h - g * g)
    cz = a + g * cu
    stores = []
    for p in range(planes):
        for j in range(tiles):
            XO[p, at(j), :] = cz * Z[p, at(j), :] - cu * U[p, at(j), :]
            RO[p, at(j), :] = B[p, at(j), :] - cz * Q[p, at(j), :] + cu * W[p, at(j), :]
        for i, (src, dst) in enumerate(((XO, x_out), (RO, r_out))):
            c = pltpu.make_async_copy(src.at[p], dst.at[p], out_sem.at[i, p])
            c.start()
            stores.append(c)
    for n, (peers, got) in enumerate(zip(groups, (g0, g1, g2))):
        if peers:
            pltpu.make_async_copy(got, got, as_sem.at[n]).wait()
    for c in sent + sent_z + sent_u:
        c.wait_send()
    for c in stores:
        c.wait()


def local(sizes, right_side, potential, permittivity, ion_mask):
    f32 = jnp.float32
    planes, rows, lanes = right_side.shape
    block = (planes, rows, lanes)
    groups = (sizes["x"] * sizes["core"], sizes["y_hi"] * sizes["y_lo"], sizes["z"])
    vm = lambda *s: pltpu.VMEM(s, f32)
    scratch = [
        vm(*block), vm(*block), vm(*block), pltpu.VMEM(block, jnp.int32),
        vm(planes - 1, rows, lanes), vm(2, rows, lanes), vm(planes, rows + 8, lanes), vm(2, planes, lanes), vm(*block),
        vm(*block), vm(*block), vm(*block), vm(*block), vm(*block), vm(*block), vm(*block), vm(*block),
        vm(3, 2, rows, lanes), vm(3, 2, planes, lanes), vm(3, 2, planes, lanes),
        vm(4, 4, 128), vm(4, 128),
    ] + [vm(max(n - 1, 1), 4, 128) for n in groups] + [
        pltpu.SemaphoreType.DMA((4,)), pltpu.SemaphoreType.DMA((2, planes)),
        pltpu.SemaphoreType.DMA((3, 4)), pltpu.SemaphoreType.DMA((3, 4)),
        pltpu.SemaphoreType.DMA((3,)), pltpu.SemaphoreType.DMA((3,)),
    ]
    any_ = pl.BlockSpec(memory_space=pl.ANY)
    return pl.pallas_call(
        functools.partial(kernel, sizes),
        out_shape=(jax.ShapeDtypeStruct(block, f32), jax.ShapeDtypeStruct(block, f32)),
        in_specs=[any_] * 4,
        out_specs=(any_, any_),
        scratch_shapes=scratch,
        compiler_params=pltpu.CompilerParams(collective_id=0, has_side_effects=True, vmem_limit_bytes=32 * 2**20),
    )(right_side, potential, permittivity, ion_mask)


def solution(mesh, sizes=SIZES):
    spec = P("gx", "yz", None)
    return jax.shard_map(functools.partial(local, sizes), mesh=mesh, in_specs=(spec,) * 4, out_specs=(spec,) * 2,
                         check_vma=False)
```

time: 404 us -> 51.8 us (0.13)
  blocking collectives: 339 us -> 0 us
  Pallas kernels: 0 us -> 45.7 us
  starting transfers between devices: 36.2 us -> 0 us
  waiting for transfers between devices: 16.6 us -> 0 us
  other arithmetic: 5.51 us -> 0 us
  between operations: 4.92 us -> 0.65 us
  local copies, waits for them, and re-layouts: 1.02 us -> 5.2 us
    psum x3 -> x0, blocking collectives: 339 us -> none  [the longest x2 227 us: preconditioned(): return lax.psum(jnp.sum(residual_now * scaled_now), ('gx', 'yz'))]
    pallas_call x0 -> x1, Pallas kernels: none -> 45.7 us  [local(): pl.pallas_call(functools.partial(kernel, sizes), out_shape=(jax.ShapeDtyp...]
    ppermute x12 -> x0, starting transfers between devices: 36.2 us -> none  [the longest x6 19.2 us: extended(): lax.ppermute(tail, axis, [(i, (i + 1) % count) for i in range(ends)])]
    ppermute x12 -> x0, waiting for transfers between devices: 16.6 us -> none  [the longest x6 16.6 us: extended(): lax.ppermute(head, axis, [((i + 1) % count, i) for i in range(ends)])]
    unnamed x10, local copies, waits for them, and re-layouts: 0.05 us -> 5.2 us
  transfers between devices with their start and end apart: 12 -> 0, of which waited for: 6 -> 0; matrix products, arithmetic and copies ran while one was open for 0% -> 0% of each run, Pallas kernels for 0% -> 0%
where the time goes in v1:
time: 51.8 us; the launch traced here: 51.5 us
  Pallas kernels  45.7 us (88%)
  local copies, waits for them, and re-layouts  5.2 us (10%)
  between operations  0.65 us (1%)
    pallas_call x1, Pallas kernels, local(): pl.pallas_call(functools.partial(kernel, sizes), out_shape=(jax.ShapeDtyp...  45.7 us
    unnamed x10, local copies, waits for them, and re-layouts  5.2 us

profile of v1, /device:TPU:1, one launch (start us, length us, event | category | flops | bytes accessed | tf_op | source)
XLA Modules:
  0.0 51.5 jit_solution(16154508678277531152)
XLA Ops:
  0.6 0.0 copy-start
  0.6 0.9 %copy-done = f32[4,32,512]{2,1,0:T(8,128)S(1)} copy-done((f32[4,32,512]{2,1,0:T(8,128)S(1)}, f32[4,32,512]{2,1,0:T(8,128)}, u32[]{:S(2)}) %copy-start) | copy-done | bytes 262168
  1.6 0.0 copy-start.1
  1.6 0.9 %copy-done.1 = f32[4,32,512]{2,1,0:T(8,128)S(1)} copy-done((f32[4,32,512]{2,1,0:T(8,128)S(1)}, f32[4,32,512]{2,1,0:T(8,128)}, u32[]{:S(2)}) %copy-start.1) | copy-done | bytes 262168
  2.5 0.0 copy-start.2
  2.5 0.9 %copy-done.2 = f32[4,32,512]{2,1,0:T(8,128)S(1)} copy-done((f32[4,32,512]{2,1,0:T(8,128)S(1)}, f32[4,32,512]{2,1,0:T(8,128)}, u32[]{:S(2)}) %copy-start.2) | copy-done | bytes 262168
  3.5 0.0 copy-start.3
  3.5 0.9 %copy-done.3 = s32[4,32,512]{2,1,0:T(8,128)S(1)} copy-done((s32[4,32,512]{2,1,0:T(8,128)S(1)}, s32[4,32,512]{2,1,0:T(8,128)}, u32[]{:S(2)}) %copy-start.3) | copy-done | bytes 262168
  4.4 45.7 %shard_map.59 = (f32[4,32,512]{2,1,0:T(8,128)S(1)}, f32[4,32,512]{2,1,0:T(8,128)S(1)}) custom-call(f32[4,32,512]{2,1,0:T(8,128)S(1)} %copy-done, f32[4,32,512]{2,1,0:T(8,128)S(1)} %copy-done.1, f32[4,32,512]{2,1,0:T(8,128)S(1)} %copy-done.2, s32[4,32,512]{2,1,0:T(8,128)S(1)} %copy-done.3), custom_call_target="tpu_custom_call" | custom-call | tf_op jit(solution)/shard_map/pallas_call | solution.py:260
  50.1 0.7 %copy.8 = f32[4,32,512]{2,1,0:T(8,128)} copy(f32[4,32,512]{2,1,0:T(8,128)S(1)} %get-tuple-element.4) | data formatting | bytes 524288
  50.8 0.7 %copy.9 = f32[4,32,512]{2,1,0:T(8,128)} copy(f32[4,32,512]{2,1,0:T(8,128)S(1)} %get-tuple-element.5) | data formatting | bytes 524288
Async XLA Ops:
  0.6 1.0 %copy-start = (f32[4,32,512]{2,1,0:T(8,128)S(1)}, f32[4,32,512]{2,1,0:T(8,128)}, u32[]{:S(2)}) copy-start(f32[4,32,512]{2,1,0:T(8,128)} %b_hbm.1) | copy-start | bytes 786436
  1.6 0.9 %copy-start.1 = (f32[4,32,512]{2,1,0:T(8,128)S(1)}, f32[4,32,512]{2,1,0:T(8,128)}, u32[]{:S(2)}) copy-start(f32[4,32,512]{2,1,0:T(8,128)} %p_hbm.1) | copy-start | bytes 786436
  2.5 0.9 %copy-start.2 = (f32[4,32,512]{2,1,0:T(8,128)S(1)}, f32[4,32,512]{2,1,0:T(8,128)}, u32[]{:S(2)}) copy-start(f32[4,32,512]{2,1,0:T(8,128)} %e_hbm.1) | copy-start | bytes 786436
  3.5 0.9 %copy-start.3 = (s32[4,32,512]{2,1,0:T(8,128)S(1)}, s32[4,32,512]{2,1,0:T(8,128)}, u32[]{:S(2)}) copy-start(s32[4,32,512]{2,1,0:T(8,128)} %m_hbm.1) | copy-start | bytes 786436

commit v2 on v1

v2 whole, which is shorter than its diff:
```python
import functools

import jax
import jax.numpy as jnp
from jax import lax
from jax.experimental import pallas as pl
from jax.experimental.pallas import tpu as pltpu
from jax.sharding import PartitionSpec as P

MESH = pl.DeviceIdType.MESH
SIZES = dict(y_hi=4, z=12, core=2, y_lo=2, x=4)


def face(a, b):
    return (2.0 * a * b) / (a + b)


def kernel(sizes, b_hbm, p_hbm, e_hbm, m_hbm, B, Z, U, Q, W, coef,
           PT, E, M, CX, CXE, CY, CZ, D0, D, RD, TS,
           XB, RB, YB, GB, RS, YS, GS, EX, T2, T4, CYH, CZH, ZH, RH, UH, ADD, CY1, Z1, R1, N1, PZ, PU,
           part, g0, g1, in_sem, hs_sem, hr_sem, as_sem, ar_sem, here):
    nyh, nz, nc, nyl, nx = (sizes[k] for k in ("y_hi", "z", "core", "y_lo", "x"))
    ngx, nyz = nyh * nz * nc, nyl * nx
    gx, yz = lax.axis_index("gx"), lax.axis_index("yz")
    core, zz, yh = gx % nc, (gx // nc) % nz, gx // (nc * nz)
    xx, yl = yz % nx, yz // nx
    ny = nyh * nyl
    yy = yh * nyl + yl
    planes, rows, lanes = E.shape
    tiles = rows // 8
    f32 = jnp.float32

    def wrap(a, n):
        return jnp.where(a >= n, a - n, a)

    xn = (jnp.where(gx > 0, gx, ngx) - 1, wrap(gx + 1, ngx))
    yn = (jnp.where(yz > 0, yz, nyz) - 1, wrap(yz + 1, nyz))
    near = [(xn[k], yz) for k in range(2)] + [(gx, yn[k]) for k in range(2)]
    near += [(xn[a], yn[b]) for a in range(2) for b in range(2)]

    def place(y, z, c, x):
        return (((y // nyl) * nz + z) * nc + c, (y % nyl) * nx + x)

    def y_rank(y):
        return jnp.where(y == 0, 0, jnp.where(2 * y <= ny, 2 * y - 1, 2 * (ny - y)))

    def y_of(r):
        return jnp.where(r % 2 == 1, (r + 1) // 2, wrap(ny - r // 2, ny))

    plane = (ny * nx, y_rank(yy) * nx + xx, lambda r: place(y_of(r // nx), zz, core, r % nx))
    column = (nz * nc, zz * nc + core, lambda r: place(yy, r // nc, r % nc, xx))
    groups = (column, plane)
    plane_peers = [place(wrap(yy + a, ny), zz, core, wrap(xx + b, nx)) for a in range(ny) for b in range(nx) if a or b]
    column_peers = [place(yy, wrap(zz + a, nz), wrap(core + b, nc), xx) for a in range(nz) for b in range(nc) if a or b]
    stages = ((column_peers, g0), (plane_peers, g1))

    def each(start, stop, act):
        lax.fori_loop(start, stop, lambda i, c: (act(i), c)[1], 0)

    barrier = pltpu.get_barrier_semaphore()
    for peer in near:
        pl.semaphore_signal(barrier, inc=1, device_id=peer, device_id_type=MESH)
    count = len(near)
    loads = [pltpu.make_async_copy(s, d, in_sem.at[i])
             for i, (s, d) in enumerate(((e_hbm, E), (p_hbm, PT), (m_hbm, M), (b_hbm, B)))]
    for c in loads:
        c.start()
    for size, rank, peer in groups:
        each(rank + 1, size, lambda r: pl.semaphore_signal(barrier, inc=1, device_id=peer(r), device_id_type=MESH))
        count = count + rank

    okx = (gx > 0, gx < ngx - 1)
    oky = (yz > 0, yz < nyz - 1)
    lane = lax.broadcasted_iota(jnp.int32, (8, lanes), 1)
    sub = lax.broadcasted_iota(jnp.int32, (8, lanes), 0)
    ends, seconds = (0, planes - 1), (1, planes - 2)
    rends, rseconds = (0, rows - 1), (1, rows - 2)

    def at(j):
        return slice(8 * j, 8 * j + 8)

    def below(j):
        return slice(8 * j + 1, 8 * j + 9)

    def before(ref, p, j):
        if j == 0:
            return pltpu.roll(ref[p, at(0), :], 1, 0)
        return ref[p, 8 * j - 1:8 * j + 7, :]

    def after(ref, p, j):
        if j == tiles - 1:
            return pltpu.roll(ref[p, at(j), :], 7, 0)
        return ref[p, below(j), :]

    def right_face(e):
        return jnp.where(lane == lanes - 1, 0.0, face(e, pltpu.roll(e, lanes - 1, 1)))

    def along_z(c, v):
        return c * pltpu.roll(v, lanes - 1, 1) + pltpu.roll(c * v, 1, 1)

    EX[...] = jnp.ones(EX.shape, f32)
    CY[:, rows:rows + 8, :] = jnp.zeros((planes, 8, lanes), f32)
    CYH[:, rows:rows + 8, :] = jnp.zeros((2, 8, lanes), f32)

    loads[0].wait()
    for p in range(planes):
        for j in range(tiles):
            e = E[p, at(j), :]
            CZ[p, at(j), :] = right_face(e)
            cy = face(e, before(E, p, j))
            CY[p, at(j), :] = jnp.where(sub == 0, 0.0, cy) if j == 0 else cy
            if p < planes - 1:
                CX[p, at(j), :] = face(e, E[p + 1, at(j), :])
    loads[1].wait()
    loads[2].wait()
    for p in range(planes):
        for j in range(tiles):
            e, cz = E[p, at(j), :], CZ[p, at(j), :]
            pt = PT[p, at(j), :]
            d = 0.25 * M[p, at(j), :].astype(f32) * (jnp.exp(pt) + jnp.exp(-pt))
            d = d + cz + pltpu.roll(cz, 1, 1) + jnp.where((lane == 0) | (lane == lanes - 1), e, 0.0)
            d = d + CY[p, at(j), :] + CY[p, below(j), :]
            if p > 0:
                d = d + CX[p - 1, at(j), :]
            if p < planes - 1:
                d = d + CX[p, at(j), :]
            D0[p, at(j), :] = d
    loads[3].wait()
    for k in range(2):
        for j in range(tiles):
            TS[k, at(j), :] = (CX[0 if k == 0 else planes - 2, at(j), :] * B[seconds[k], at(j), :]
                               / D0[seconds[k], at(j), :])
        for n, ref in enumerate((E, B, D0)):
            for m in range(2):
                RS[k, 2 * n + m:2 * n + m + 1, :] = ref[seconds[k], rends[m]:rends[m] + 1, :]
                GS[k, m, n:n + 1, :] = ref[ends[k], rends[m]:rends[m] + 1, :]
            YS[k, n] = ref[:, rends[k], :]
            YS[k, 3 + n] = ref[:, rseconds[k], :]
        for m in range(2):
            GS[k, m, 3:4, :] = E[seconds[k], rends[m]:rends[m] + 1, :]
            GS[k, m, 4:5, :] = E[ends[k], rseconds[m]:rseconds[m] + 1, :]

    pl.semaphore_wait(barrier, count)
    plan = []
    for n, ref in enumerate((E, B, D0, TS)):
        for k in range(2):
            src = ref.at[k] if n == 3 else ref.at[ends[k]]
            plan.append((src, XB.at[1 - k, n], (xn[k], yz)))
    for k in range(2):
        plan.append((YS.at[k], YB.at[1 - k], (gx, yn[k])))
        plan.append((RS.at[k], RB.at[1 - k], (xn[k], yz)))
        for m in range(2):
            plan.append((GS.at[k, m], GB.at[1 - k, 1 - m], (xn[k], yn[m])))
    sent = []
    for n, (src, dst, dev) in enumerate(plan):
        c = pltpu.make_async_remote_copy(src_ref=src, dst_ref=dst, send_sem=hs_sem.at[n], recv_sem=hr_sem.at[n],
                                         device_id=dev, device_id_type=MESH)
        c.start()
        sent.append(c)
    for n, (size, rank, peer) in enumerate(groups):
        each(0, rank, lambda r: pl.semaphore_signal(here.at[n], inc=1, device_id=peer(r), device_id_type=MESH))
    for c in sent:
        c.wait_recv()

    last = planes + 1
    for m in range(2):
        for n, (row, corner) in enumerate(((0, 0), (1, 1), (2, 2), (3, 4), (4, None), (5, None))):
            EX[m, n, 1:last, :] = YB[m, row]
            if corner is not None:
                EX[m, n, 0:1, :] = GB[0, m, corner:corner + 1, :]
                EX[m, n, last:last + 1, :] = GB[1, m, corner:corner + 1, :]
        EX[m, 6, 0:1, :] = XB[0, 0, rends[m]:rends[m] + 1, :]
        EX[m, 6, 1:last, :] = E[:, rends[m], :]
        EX[m, 6, last:last + 1, :] = XB[1, 0, rends[m]:rends[m] + 1, :]
        e1, b1, p1, e2, b2, p2, e0 = (EX[m, n] for n in range(7))

        def crossing(e, outer):
            lo = face(e, pltpu.roll(e, 1, 0))
            hi = pltpu.roll(lo, 7, 0)
            a_lo, a_hi = jnp.where(okx[0], lo, e), jnp.where(okx[1], hi, e)
            add = jnp.where(sub == 1, a_lo, 0.0) + jnp.where(sub == last - 1, a_hi, 0.0)
            if outer:
                add = add + jnp.where(sub == 0, jnp.where(okx[0], hi, e), 0.0)
                add = add + jnp.where(sub == last, jnp.where(okx[1], lo, e), 0.0)
            return lo, add

        lo, add = crossing(e1, True)
        lo = jnp.where(sub == 1, jnp.where(okx[0], lo, 0.0), lo)
        lo = jnp.where(sub == last, jnp.where(okx[1], lo, 0.0), lo)
        fy = face(e1, e0)
        cy = jnp.where(oky[m], fy, 0.0)
        r1 = 1.0 / (p1 + add + jnp.where(oky[m], fy, e1))
        z1 = b1 * r1
        t = face(e1, e2) * b2 / (p2 + crossing(e2, False)[1])
        t = t + along_z(right_face(e1), z1)
        t = t + lo * pltpu.roll(z1, 1, 0) + pltpu.roll(lo, 7, 0) * pltpu.roll(z1, 7, 0)
        ADD[m] = jnp.where(oky[m], fy, e0)
        CY1[m], Z1[m], R1[m], N1[m], PZ[m] = cy, z1, r1, t, cy * z1
        for k in range(2):
            T2[k, 0, m:m + 1, :] = XB[k, 0, rends[m]:rends[m] + 1, :]
            T2[k, 1, m:m + 1, :] = GB[k, m, 3:4, :]
    for k in range(2):
        e1, ed = T2[k, 0], T2[k, 1]
        e2, b2, d2 = RB[k, 0:2, :], RB[k, 2:4, :], RB[k, 4:6, :]
        f = face(e2, ed)
        row2 = lax.broadcasted_iota(jnp.int32, (2, lanes), 0)
        f = jnp.where(row2 == 0, jnp.where(oky[0], f, e2), jnp.where(oky[1], f, e2))
        T4[k] = face(e1, e2) * b2 / (d2 + f)

    def end_rows(j, p1, ref, k0=0):
        t = 0.0
        if j == 0:
            t = t + jnp.where(sub == 0, ref[0, p1:p1 + 1, :], 0.0)
        if j == tiles - 1:
            t = t + jnp.where(sub == 7, ref[1, p1:p1 + 1, :], 0.0)
        return t

    for k, p in enumerate(ends):
        h = last * k
        for j in range(tiles):
            e, eh = E[p, at(j), :], XB[k, 0, at(j), :]
            fx = face(e, eh)
            CXE[k, at(j), :] = jnp.where(okx[k], fx, 0.0)
            d = D0[p, at(j), :] + jnp.where(okx[k], fx, e)
            dh = XB[k, 2, at(j), :] + jnp.where(okx[k], fx, eh)
            if j in (0, tiles - 1):
                d = d + end_rows(j, p + 1, ADD)
                dh = dh + end_rows(j, h, ADD)
            rd, rh = 1.0 / d, 1.0 / dh
            D[p, at(j), :] = d
            RD[p, at(j), :] = rd
            Z[p, at(j), :] = B[p, at(j), :] * rd
            RH[k, at(j), :] = rh
            ZH[k, at(j), :] = XB[k, 1, at(j), :] * rh
            CZH[k, at(j), :] = right_face(eh)
            cy = face(eh, before(XB.at[k], 0, j))
            CYH[k, at(j), :] = jnp.where(sub == 0, 0.0, cy) if j == 0 else cy
    for p in range(1, planes - 1):
        for j in range(tiles):
            d = D0[p, at(j), :]
            if j in (0, tiles - 1):
                d = d + end_rows(j, p + 1, ADD)
            rd = 1.0 / d
            D[p, at(j), :] = d
            RD[p, at(j), :] = rd
            Z[p, at(j), :] = B[p, at(j), :] * rd

    def image(V, VH, PV, p, j):
        v = V[p, at(j), :]
        t = D[p, at(j), :] * v - along_z(CZ[p, at(j), :], v)
        t = t - CY[p, at(j), :] * before(V, p, j) - CY[p, below(j), :] * after(V, p, j)
        if p > 0:
            t = t - CX[p - 1, at(j), :] * V[p - 1, at(j), :]
        else:
            t = t - CXE[0, at(j), :] * VH[0, at(j), :]
        if p < planes - 1:
            t = t - CX[p, at(j), :] * V[p + 1, at(j), :]
        else:
            t = t - CXE[1, at(j), :] * VH[1, at(j), :]
        if j in (0, tiles - 1):
            t = t - end_rows(j, p + 1, PV)
        return t

    s0 = s1 = s2 = s3 = jnp.zeros((8, lanes), f32)
    for p in range(planes):
        for j in range(tiles):
            z = Z[p, at(j), :]
            q = image(Z, ZH, PZ, p, j)
            u = q * RD[p, at(j), :]
            Q[p, at(j), :] = q
            U[p, at(j), :] = u
            s0 = s0 + B[p, at(j), :] * z
            s1 = s1 + z * q
            s2 = s2 + q * u
    for m in range(2):
        EX[m, 7, 1:last, :] = Z[:, rends[m], :]
        t = N1[m] + CY1[m] * EX[m, 7]
        PU[m] = CY1[m] * (Z1[m] - t * R1[m])
    for k, p in enumerate(ends):
        h = last * k
        for j in range(tiles):
            v = ZH[k, at(j), :]
            t = XB[k, 3, at(j), :]
            if j == 0:
                t = jnp.where(sub == 0, T4[k, 0:1, :], t)
            if j == tiles - 1:
                t = jnp.where(sub == 7, T4[k, 1:2, :], t)
            t = t + CXE[k, at(j), :] * Z[p, at(j), :] + along_z(CZH[k, at(j), :], v)
            t = t + CYH[k, at(j), :] * before(ZH, k, j) + CYH[k, below(j), :] * after(ZH, k, j)
            if j in (0, tiles - 1):
                t = t + end_rows(j, h, PZ)
            UH[k, at(j), :] = v - t * RH[k, at(j), :]
    for p in range(planes):
        for j in range(tiles):
            w = image(U, UH, PU, p, j)
            W[p, at(j), :] = w
            s3 = s3 + U[p, at(j), :] * w

    def folded(s):
        t = s[:, :128]
        for i in range(128, lanes, 128):
            t = t + s[:, i:i + 128]
        return jnp.sum(t, axis=0, keepdims=True)

    lane1 = lax.broadcasted_iota(jnp.int32, (1, 128), 1)
    message = jnp.zeros((1, 128), f32)
    for k, t in enumerate((s0, s1, s2, s3)):
        t = folded(t)
        t = t + pltpu.roll(t, 64, 1)
        t = t + pltpu.roll(t, 32, 1)
        message = jnp.where(lane1 // 32 == k, t, message)
    part[0] = message
    for n, ((peers, got), (size, rank, peer)) in enumerate(zip(stages, groups)):
        @pl.when(rank < size - 1)
        def _():
            pl.semaphore_wait(here.at[n], size - 1 - rank)

        for d, dev in enumerate(peers):
            pltpu.make_async_remote_copy(src_ref=part.at[n], dst_ref=got.at[d], send_sem=as_sem.at[n],
                                         recv_sem=ar_sem.at[n], device_id=dev, device_id_type=MESH).start()
        total = part[n]
        if peers:
            pltpu.make_async_copy(got, got, ar_sem.at[n]).wait()
            for d in range(len(peers)):
                total = total + got[d]
        part[n + 1] = total
    row4 = lax.broadcasted_iota(jnp.int32, (4, 128), 0)
    lane4 = lax.broadcasted_iota(jnp.int32, (4, 128), 1)
    s = jnp.sum(jnp.where(lane4 // 32 == row4, part[2], 0.0), axis=1, keepdims=True)
    s0, s1, s2, s3 = s[0:1], s[1:2], s[2:3], s[3:4]
    a, g, h = s0 / s1, s2 / s1, s3 / s1
    cu = (a * g - 1.0) / (h - g * g)
    cz = a + g * cu
    coef[0:1, :] = jnp.broadcast_to(cz, (1, 128))
    coef[1:2, :] = jnp.broadcast_to(cu, (1, 128))
    for n, (peers, got) in enumerate(stages):
        if peers:
            pltpu.make_async_copy(got, got, as_sem.at[n]).wait()
    for d in sent:
        d.wait_send()


def local(sizes, right_side, potential, permittivity, ion_mask):
    f32 = jnp.float32
    planes, rows, lanes = block = right_side.shape
    columns, in_plane = sizes["z"] * sizes["core"], sizes["x"] * sizes["y_hi"] * sizes["y_lo"]
    vm = lambda *s: pltpu.VMEM(s, f32)
    full, pad = vm(*block), vm(2, 8, lanes)
    side = vm(2, rows, lanes)
    scratch = [
        full, full, pltpu.VMEM(block, jnp.int32),
        vm(planes - 1, rows, lanes), side, vm(planes, rows + 8, lanes), full, full, full, full, side,
        vm(2, 4, rows, lanes), vm(2, 8, lanes), vm(2, 6, planes, lanes), vm(2, 2, 8, lanes),
        vm(2, 8, lanes), vm(2, 6, planes, lanes), vm(2, 2, 8, lanes),
        vm(2, 8, 8, lanes), vm(2, 2, 2, lanes), vm(2, 2, lanes),
        vm(2, rows + 8, lanes), side, side, side, side, pad, pad, pad, pad, pad, pad, pad,
        vm(3, 1, 128), vm(max(columns - 1, 1), 1, 128), vm(max(in_plane - 1, 1), 1, 128),
        pltpu.SemaphoreType.DMA((4,)),
        pltpu.SemaphoreType.DMA((16,)), pltpu.SemaphoreType.DMA((16,)),
        pltpu.SemaphoreType.DMA((2,)), pltpu.SemaphoreType.DMA((2,)), pltpu.SemaphoreType.REGULAR((2,)),
    ]
    hbm, vmem = pl.BlockSpec(memory_space=pltpu.HBM), pl.BlockSpec(memory_space=pltpu.VMEM)
    args = (right_side, potential, permittivity, ion_mask)
    whole = jax.ShapeDtypeStruct(block, f32)
    fields = pl.pallas_call(
        functools.partial(kernel, sizes),
        out_shape=(whole,) * 5 + (jax.ShapeDtypeStruct((2, 128), f32),),
        in_specs=[hbm] * 4,
        out_specs=(vmem,) * 6,
        scratch_shapes=scratch,
        compiler_params=pltpu.CompilerParams(collective_id=0, has_side_effects=True, vmem_limit_bytes=24 * 2**20),
    )(*[pltpu.with_memory_space_constraint(a, pltpu.HBM) for a in args])
    return pl.pallas_call(
        finish,
        out_shape=(whole, whole),
        in_specs=[vmem] * 6,
        out_specs=(hbm, hbm),
        scratch_shapes=[full, full, pltpu.SemaphoreType.DMA((2, planes))],
        compiler_params=pltpu.CompilerParams(vmem_limit_bytes=16 * 2**20),
    )(*fields)


def finish(B, Z, U, Q, W, coef, x_out, r_out, X, R, sem):
    cz, cu = coef[0:1, 0:1], coef[1:2, 0:1]
    stores = []
    for p in range(B.shape[0]):
        X[p] = cz * Z[p] - cu * U[p]
        R[p] = B[p] - cz * Q[p] + cu * W[p]
        for i, (src, dst) in enumerate(((X, x_out), (R, r_out))):
            c = pltpu.make_async_copy(src.at[p], dst.at[p], sem.at[i, p])
            c.start()
            stores.append(c)
    for c in stores:
        c.wait()


def solution(mesh, sizes=SIZES):
    spec = P("gx", "yz", None)
    return jax.shard_map(functools.partial(local, sizes), mesh=mesh, in_specs=(spec,) * 4, out_specs=(spec,) * 2,
                         check_vma=False)
```

time: 51.8 us -> 42.4 us (0.82)
  local copies, waits for them, and re-layouts: 5.2 us -> 0 us
  Pallas kernels: 45.7 us -> 41.7 us
    unnamed x10 -> x0, local copies, waits for them, and re-layouts: 5.2 us -> none
    pallas_call x1 -> x2, Pallas kernels: 45.7 us -> 41.7 us  [the longest x1 40.8 us: local(): pl.pallas_call(functools.partial(kernel, sizes), out_shape=(whole,) * 5 +...]
where the time goes in v2:
time: 42.4 us; the launch traced here: 42.3 us
  Pallas kernels  41.7 us (98%)
  between operations  0.64 us (2%)
    pallas_call x1, Pallas kernels, local(): pl.pallas_call(functools.partial(kernel, sizes), out_shape=(whole,) * 5 +...  40.8 us
    pallas_call x1, Pallas kernels, local(): pl.pallas_call(finish, out_shape=(whole, whole), in_specs=[vmem] * 6, out...  0.9 us

profile of v2, /device:TPU:1, one launch (start us, length us, event | category | flops | bytes accessed | tf_op | source)
XLA Modules:
  0.0 42.3 jit_solution(17378131677498722806)
XLA Ops:
  0.6 40.8 %shard_map.59 = (f32[4,32,512]{2,1,0:T(8,128)S(1)}, f32[4,32,512]{2,1,0:T(8,128)S(1)}, f32[4,32,512]{2,1,0:T(8,128)S(1)}, f32[4,32,512]{2,1,0:T(8,128)S(1)}, f32...) custom-call(f32[4,32,512]{2,1,0:T(8,128)} %b_hbm.1, f32[4,32,512]{2,1,0:T(8,128)} %p_hbm.1, f32[4,32,512]{2,1,0:T(8,128)} %e_hbm.1, ...), custom_call_target="tpu_custom_call" | custom-call | tf_op jit(solution)/shard_map/pallas_call | solution.py:365
  41.4 0.9 %shard_map.60 = (f32[4,32,512]{2,1,0:T(8,128)}, f32[4,32,512]{2,1,0:T(8,128)}) custom-call(f32[4,32,512]{2,1,0:T(8,128)S(1)} %get-tuple-element.8.B, f32[4,32,512]{2,1,0:T(8,128)S(1)} %get-tuple-element.9.Z, f32[4,32,512]{2,1,0:T(8,128)S(1)} %get-tuple-element.10.U, f32[4,32,512]{2,1,0:T(8,128)S(1)} %get-tuple-element.11.Q, ...), custom_call_target="tpu_custom_call" | custom-call | tf_op jit(solution)/shard_map/pallas_call | solution.py:373

commit v3 on v2

--- a/solution.py
+++ b/solution.py
@@ -15,15 +15,24 @@
     return (2.0 * a * b) / (a + b)
 
 
+def div(a, n):
+    return a >> (n.bit_length() - 1) if n & (n - 1) == 0 else lax.div(a, jnp.int32(n))
+
+
+def mod(a, n):
+    return a & (n - 1) if n & (n - 1) == 0 else a - div(a, n) * n
+
+
 def kernel(sizes, b_hbm, p_hbm, e_hbm, m_hbm, B, Z, U, Q, W, coef,
            PT, E, M, CX, CXE, CY, CZ, D0, D, RD, TS,
-           XB, RB, YB, GB, RS, YS, GS, EX, T2, T4, CYH, CZH, ZH, RH, UH, ADD, CY1, Z1, R1, N1, PZ, PU,
-           part, g0, g1, in_sem, hs_sem, hr_sem, as_sem, ar_sem, here):
+           XB, RB, YB, RS, YS, EX, T2, T4, CYH, CZH, ZH, RH, UH, ADD, CY1, Z1, R1, N1, PZ, PU,
+           part, g0, g1, in_sem, hs_sem, hr_sem, as_sem, ar_sem, here, close):
     nyh, nz, nc, nyl, nx = (sizes[k] for k in ("y_hi", "z", "core", "y_lo", "x"))
     ngx, nyz = nyh * nz * nc, nyl * nx
     gx, yz = lax.axis_index("gx"), lax.axis_index("yz")
-    core, zz, yh = gx % nc, (gx // nc) % nz, gx // (nc * nz)
-    xx, yl = yz % nx, yz // nx
+    core, yh = mod(gx, nc), div(gx, nz * nc)
+    zz = div(gx - yh * (nz * nc), nc)
+    xx, yl = mod(yz, nx), div(yz, nx)
     ny = nyh * nyl
     yy = yh * nyl + yl
     planes, rows, lanes = E.shape
@@ -36,41 +45,70 @@
     xn = (jnp.where(gx > 0, gx, ngx) - 1, wrap(gx + 1, ngx))
     yn = (jnp.where(yz > 0, yz, nyz) - 1, wrap(yz + 1, nyz))
     near = [(xn[k], yz) for k in range(2)] + [(gx, yn[k]) for k in range(2)]
-    near += [(xn[a], yn[b]) for a in range(2) for b in range(2)]
 
     def place(y, z, c, x):
-        return (((y // nyl) * nz + z) * nc + c, (y % nyl) * nx + x)
+        return ((div(y, nyl) * nz + z) * nc + c, mod(y, nyl) * nx + x)
 
     def y_rank(y):
         return jnp.where(y == 0, 0, jnp.where(2 * y <= ny, 2 * y - 1, 2 * (ny - y)))
 
-    def y_of(r):
-        return jnp.where(r % 2 == 1, (r + 1) // 2, wrap(ny - r // 2, ny))
-
-    plane = (ny * nx, y_rank(yy) * nx + xx, lambda r: place(y_of(r // nx), zz, core, r % nx))
-    column = (nz * nc, zz * nc + core, lambda r: place(yy, r // nc, r % nc, xx))
-    groups = (column, plane)
-    plane_peers = [place(wrap(yy + a, ny), zz, core, wrap(xx + b, nx)) for a in range(ny) for b in range(nx) if a or b]
+    column_rank, my_y = zz * nc + core, y_rank(yy)
+    my_plane = my_y * nx + xx
+    y_order = sorted(range(ny), key=lambda y: min(y, ny - y) * 2 + (2 * y > ny))
+    sizes_ranks = ((nz * nc, column_rank), (ny * nx, my_plane))
+
+    def far(a, n):
+        return min(a, n - a)
+
+    offsets = sorted(((a, b) for a in range(ny) for b in range(nx) if a or b), key=lambda o: -far(o[0], ny) - far(o[1], nx))
+    plane_peers = [place(wrap(yy + a, ny), zz, core, wrap(xx + b, nx)) for a, b in offsets]
     column_peers = [place(yy, wrap(zz + a, nz), wrap(core + b, nc), xx) for a in range(nz) for b in range(nc) if a or b]
     stages = ((column_peers, g0), (plane_peers, g1))
 
+    def signal(sem, dev):
+        pl.semaphore_signal(sem, inc=1, device_id=dev, device_id_type=MESH)
+
     def each(start, stop, act):
         lax.fori_loop(start, stop, lambda i, c: (act(i), c)[1], 0)
 
-    barrier = pltpu.get_barrier_semaphore()
-    for peer in near:
-        pl.semaphore_signal(barrier, inc=1, device_id=peer, device_id_type=MESH)
-    count = len(near)
+    def group_signals(sems, later):
+        base = gx - column_rank
+        if later:
+            each(column_rank + 1, nz * nc, lambda r: signal(sems[0], (base + r, yz)))
+        else:
+            each(0, column_rank, lambda r: signal(sems[0], (base + r, yz)))
+        for r, y in enumerate(y_order):
+            g, q = (y // nyl) * nz * nc + column_rank, (y % nyl) * nx
+
+            @pl.when(r > my_y if later else r < my_y)
+            def _():
+                for x in range(nx):
+                    signal(sems[1], (g, q + x))
+
+        if later:
+            each(xx + 1, nx, lambda x: signal(sems[1], (gx, yl * nx + x)))
+        else:
+            each(0, xx, lambda x: signal(sems[1], (gx, yl * nx + x)))
+
+    okx = (gx > 0, gx < ngx - 1)
+    oky = (yz > 0, yz < nyz - 1)
+    earlier = [column_rank > 0, column_rank == nz * nc - 1]
+    earlier += [y_rank(yh * nyl + div(q, nx)) * nx + mod(q, nx) < my_plane for q in yn]
+    mirror = (1, 0, 3, 2)
+    ok = okx + oky
+    later = [jnp.logical_and(ok[n], jnp.logical_not(earlier[n])) for n in range(4)]
+    earlier = [jnp.logical_and(ok[n], earlier[n]) for n in range(4)]
     loads = [pltpu.make_async_copy(s, d, in_sem.at[i])
              for i, (s, d) in enumerate(((e_hbm, E), (p_hbm, PT), (m_hbm, M), (b_hbm, B)))]
     for c in loads:
         c.start()
-    for size, rank, peer in groups:
-        each(rank + 1, size, lambda r: pl.semaphore_signal(barrier, inc=1, device_id=peer(r), device_id_type=MESH))
-        count = count + rank
-
-    okx = (gx > 0, gx < ngx - 1)
-    oky = (yz > 0, yz < nyz - 1)
+    barrier = pltpu.get_barrier_semaphore()
+    count = column_rank + my_plane
+    for n, dev in enumerate(near):
+        pl.when(later[n])(functools.partial(signal, barrier, dev))
+        count = count + jnp.where(earlier[n], 1, 0)
+    group_signals((barrier, barrier), True)
+
     lane = lax.broadcasted_iota(jnp.int32, (8, lanes), 1)
     sub = lax.broadcasted_iota(jnp.int32, (8, lanes), 0)
     ends, seconds = (0, planes - 1), (1, planes - 2)
@@ -98,9 +136,22 @@
     def along_z(c, v):
         return c * pltpu.roll(v, lanes - 1, 1) + pltpu.roll(c * v, 1, 1)
 
+    for n in range(4):
+        @pl.when(jnp.logical_not(ok[n]))
+        def _():
+            for ref in ((XB, RB) if n < 2 else (YB,)):
+                ref[n % 2] = jnp.ones(ref.shape[1:], f32)
+
     EX[...] = jnp.ones(EX.shape, f32)
     CY[:, rows:rows + 8, :] = jnp.zeros((planes, 8, lanes), f32)
     CYH[:, rows:rows + 8, :] = jnp.zeros((2, 8, lanes), f32)
+
+    @pl.when(count > 0)
+    def _():
+        pl.semaphore_wait(barrier, count)
+
+    for n, dev in enumerate(near):
+        pl.when(earlier[n])(functools.partial(signal, close.at[mirror[n]], dev))
 
     loads[0].wait()
     for p in range(planes):
@@ -133,42 +184,65 @@
         for n, ref in enumerate((E, B, D0)):
             for m in range(2):
                 RS[k, 2 * n + m:2 * n + m + 1, :] = ref[seconds[k], rends[m]:rends[m] + 1, :]
-                GS[k, m, n:n + 1, :] = ref[ends[k], rends[m]:rends[m] + 1, :]
             YS[k, n] = ref[:, rends[k], :]
             YS[k, 3 + n] = ref[:, rseconds[k], :]
+
+    plan = [[] for _ in near]
+    for k in range(2):
+        plan[2 + k].append((YS.at[k], YB.at[1 - k]))
+        for n, ref in enumerate((E, B, D0, TS)):
+            plan[k].append((ref.at[k] if n == 3 else ref.at[ends[k]], XB.at[1 - k, n]))
+        plan[k].append((RS.at[k], RB.at[1 - k]))
+    total, sent = 0, [[] for _ in near]
+    for n, dev in enumerate(near):
+        for src, dst in plan[n]:
+            sent[n].append(pltpu.make_async_remote_copy(
+                src_ref=src, dst_ref=dst, send_sem=hs_sem.at[total], recv_sem=hr_sem.at[total],
+                device_id=dev, device_id_type=MESH))
+            total += 1
+    order = (2, 3, 1, 0)
+
+    def send(n):
+        for c in sent[n][:4]:
+            c.start()
+
+    def send_later(n):
+        pl.semaphore_wait(close.at[n], 1)
+        send(n)
+
+    for n in order:
+        pl.when(earlier[n])(functools.partial(send, n))
+    group_signals((here.at[0], here.at[1]), False)
+    for n in order[:3]:
+        pl.when(later[n])(functools.partial(send_later, n))
+
+    for n in (2, 3):
+        pl.when(ok[mirror[n]])(sent[n][0].wait_recv)
+    for k in range(2):
         for m in range(2):
-            GS[k, m, 3:4, :] = E[seconds[k], rends[m]:rends[m] + 1, :]
-            GS[k, m, 4:5, :] = E[ends[k], rseconds[m]:rseconds[m] + 1, :]
-
-    pl.semaphore_wait(barrier, count)
-    plan = []
-    for n, ref in enumerate((E, B, D0, TS)):
-        for k in range(2):
-            src = ref.at[k] if n == 3 else ref.at[ends[k]]
-            plan.append((src, XB.at[1 - k, n], (xn[k], yz)))
-    for k in range(2):
-        plan.append((YS.at[k], YB.at[1 - k], (gx, yn[k])))
-        plan.append((RS.at[k], RB.at[1 - k], (xn[k], yz)))
-        for m in range(2):
-            plan.append((GS.at[k, m], GB.at[1 - k, 1 - m], (xn[k], yn[m])))
-    sent = []
-    for n, (src, dst, dev) in enumerate(plan):
-        c = pltpu.make_async_remote_copy(src_ref=src, dst_ref=dst, send_sem=hs_sem.at[n], recv_sem=hr_sem.at[n],
-                                         device_id=dev, device_id_type=MESH)
-        c.start()
-        sent.append(c)
-    for n, (size, rank, peer) in enumerate(groups):
-        each(0, rank, lambda r: pl.semaphore_signal(here.at[n], inc=1, device_id=peer(r), device_id_type=MESH))
-    for c in sent:
-        c.wait_recv()
+            for n, (row, p) in enumerate(((0, ends[k]), (1, ends[k]), (2, ends[k]), (0, seconds[k]), (3, ends[k]))):
+                RS[k, 6 + 5 * m + n:7 + 5 * m + n, :] = YB[m, row, p:p + 1, :]
+    pl.when(ok[1])(sent[1][4].start)
+
+    @pl.when(later[0])
+    def _():
+        pl.semaphore_wait(close.at[0], 1)
+
+    pl.when(ok[0])(sent[0][4].start)
+    pl.when(later[0])(functools.partial(send, 0))
+    for n in (1, 0):
+        @pl.when(ok[mirror[n]])
+        def _():
+            for c in (*sent[n][:3], sent[n][4]):
+                c.wait_recv()
 
     last = planes + 1
     for m in range(2):
         for n, (row, corner) in enumerate(((0, 0), (1, 1), (2, 2), (3, 4), (4, None), (5, None))):
             EX[m, n, 1:last, :] = YB[m, row]
             if corner is not None:
-                EX[m, n, 0:1, :] = GB[0, m, corner:corner + 1, :]
-                EX[m, n, last:last + 1, :] = GB[1, m, corner:corner + 1, :]
+                EX[m, n, 0:1, :] = RB[0, 6 + 5 * m + corner:7 + 5 * m + corner, :]
+                EX[m, n, last:last + 1, :] = RB[1, 6 + 5 * m + corner:7 + 5 * m + corner, :]
         EX[m, 6, 0:1, :] = XB[0, 0, rends[m]:rends[m] + 1, :]
         EX[m, 6, 1:last, :] = E[:, rends[m], :]
         EX[m, 6, last:last + 1, :] = XB[1, 0, rends[m]:rends[m] + 1, :]
@@ -198,7 +272,7 @@
         CY1[m], Z1[m], R1[m], N1[m], PZ[m] = cy, z1, r1, t, cy * z1
         for k in range(2):
             T2[k, 0, m:m + 1, :] = XB[k, 0, rends[m]:rends[m] + 1, :]
-            T2[k, 1, m:m + 1, :] = GB[k, m, 3:4, :]
+            T2[k, 1, m:m + 1, :] = RB[k, 9 + 5 * m:10 + 5 * m, :]
     for k in range(2):
         e1, ed = T2[k, 0], T2[k, 1]
         e2, b2, d2 = RB[k, 0:2, :], RB[k, 2:4, :], RB[k, 4:6, :]
@@ -276,6 +350,8 @@
         EX[m, 7, 1:last, :] = Z[:, rends[m], :]
         t = N1[m] + CY1[m] * EX[m, 7]
         PU[m] = CY1[m] * (Z1[m] - t * R1[m])
+    for n in range(2):
+        pl.when(ok[mirror[n]])(sent[n][3].wait_recv)
     for k, p in enumerate(ends):
         h = last * k
         for j in range(tiles):
@@ -310,7 +386,7 @@
         t = t + pltpu.roll(t, 32, 1)
         message = jnp.where(lane1 // 32 == k, t, message)
     part[0] = message
-    for n, ((peers, got), (size, rank, peer)) in enumerate(zip(stages, groups)):
+    for n, ((peers, got), (size, rank)) in enumerate(zip(stages, sizes_ranks)):
         @pl.when(rank < size - 1)
         def _():
             pl.semaphore_wait(here.at[n], size - 1 - rank)
@@ -336,8 +412,11 @@
     for n, (peers, got) in enumerate(stages):
         if peers:
             pltpu.make_async_copy(got, got, as_sem.at[n]).wait()
-    for d in sent:
-        d.wait_send()
+    for n in range(4):
+        @pl.when(ok[n])
+        def _():
+            for c in sent[n]:
+                c.wait_send()
 
 
 def local(sizes, right_side, potential, permittivity, ion_mask):
@@ -350,14 +429,14 @@
     scratch = [
         full, full, pltpu.VMEM(block, jnp.int32),
         vm(planes - 1, rows, lanes), side, vm(planes, rows + 8, lanes), full, full, full, full, side,
-        vm(2, 4, rows, lanes), vm(2, 8, lanes), vm(2, 6, planes, lanes), vm(2, 2, 8, lanes),
-        vm(2, 8, lanes), vm(2, 6, planes, lanes), vm(2, 2, 8, lanes),
+        vm(2, 4, rows, lanes), vm(2, 16, lanes), vm(2, 6, planes, lanes), vm(2, 16, lanes), vm(2, 6, planes, lanes),
         vm(2, 8, 8, lanes), vm(2, 2, 2, lanes), vm(2, 2, lanes),
         vm(2, rows + 8, lanes), side, side, side, side, pad, pad, pad, pad, pad, pad, pad,
         vm(3, 1, 128), vm(max(columns - 1, 1), 1, 128), vm(max(in_plane - 1, 1), 1, 128),
         pltpu.SemaphoreType.DMA((4,)),
-        pltpu.SemaphoreType.DMA((16,)), pltpu.SemaphoreType.DMA((16,)),
+        pltpu.SemaphoreType.DMA((12,)), pltpu.SemaphoreType.DMA((12,)),
         pltpu.SemaphoreType.DMA((2,)), pltpu.SemaphoreType.DMA((2,)), pltpu.SemaphoreType.REGULAR((2,)),
+        pltpu.SemaphoreType.REGULAR((4,)),
     ]
     hbm, vmem = pl.BlockSpec(memory_space=pltpu.HBM), pl.BlockSpec(memory_space=pltpu.VMEM)
     args = (right_side, potential, permittivity, ion_mask)

time: 42.4 us -> 41.3 us (0.974)
  Pallas kernels: 41.7 us -> 40.5 us
    pallas_call x1, Pallas kernels: 40.8 us -> 39.6 us  [local(): pl.pallas_call(functools.partial(kernel, sizes), out_shape=(whole,) * 5 +...]
where the time goes in v3:
time: 41.3 us; the launch traced here: 41.2 us
  Pallas kernels  40.5 us (98%)
  between operations  0.64 us (2%)
    pallas_call x1, Pallas kernels, local(): pl.pallas_call(functools.partial(kernel, sizes), out_shape=(whole,) * 5 +...  39.6 us
    pallas_call x1, Pallas kernels, local(): pl.pallas_call(finish, out_shape=(whole, whole), in_specs=[vmem] * 6, out...  0.9 us

profile of v3, /device:TPU:1, one launch (start us, length us, event | category | flops | bytes accessed | tf_op | source)
XLA Modules:
  0.0 41.2 jit_solution(2868128477617952072)
XLA Ops:
  0.6 39.6 %shard_map.59 = (f32[4,32,512]{2,1,0:T(8,128)S(1)}, f32[4,32,512]{2,1,0:T(8,128)S(1)}, f32[4,32,512]{2,1,0:T(8,128)S(1)}, f32[4,32,512]{2,1,0:T(8,128)S(1)}, f32...) custom-call(f32[4,32,512]{2,1,0:T(8,128)} %b_hbm.1, f32[4,32,512]{2,1,0:T(8,128)} %p_hbm.1, f32[4,32,512]{2,1,0:T(8,128)} %e_hbm.1, ...), custom_call_target="tpu_custom_call" | custom-call | tf_op jit(solution)/shard_map/pallas_call | solution.py:444
  40.3 0.9 %shard_map.60 = (f32[4,32,512]{2,1,0:T(8,128)}, f32[4,32,512]{2,1,0:T(8,128)}) custom-call(f32[4,32,512]{2,1,0:T(8,128)S(1)} %get-tuple-element.8.B, f32[4,32,512]{2,1,0:T(8,128)S(1)} %get-tuple-element.9.Z, f32[4,32,512]{2,1,0:T(8,128)S(1)} %get-tuple-element.10.U, f32[4,32,512]{2,1,0:T(8,128)S(1)} %get-tuple-element.11.Q, ...), custom_call_target="tpu_custom_call" | custom-call | tf_op jit(solution)/shard_map/pallas_call | solution.py:452

commit v4 on v3

--- a/solution.py
+++ b/solution.py
@@ -187,6 +187,7 @@
             YS[k, n] = ref[:, rends[k], :]
             YS[k, 3 + n] = ref[:, rseconds[k], :]
 
+    group_signals((here.at[0], here.at[1]), False)
     plan = [[] for _ in near]
     for k in range(2):
         plan[2 + k].append((YS.at[k], YB.at[1 - k]))
@@ -212,7 +213,6 @@
 
     for n in order:
         pl.when(earlier[n])(functools.partial(send, n))
-    group_signals((here.at[0], here.at[1]), False)
     for n in order[:3]:
         pl.when(later[n])(functools.partial(send_later, n))
 

time: 41.3 us -> 41.3 us (level)
  no operation moved by 1% of the time
where the time goes in v4:
time: 41.3 us; the launch traced here: 41.2 us
  Pallas kernels  40.5 us (98%)
  between operations  0.64 us (2%)
    pallas_call x1, Pallas kernels, local(): pl.pallas_call(functools.partial(kernel, sizes), out_shape=(whole,) * 5 +...  39.6 us
    pallas_call x1, Pallas kernels, local(): pl.pallas_call(finish, out_shape=(whole, whole), in_specs=[vmem] * 6, out...  0.9 us

profile of v4, /device:TPU:1, one launch (start us, length us, event | category | flops | bytes accessed | tf_op | source)
XLA Modules:
  0.0 41.2 jit_solution(15959493903807237390)
XLA Ops:
  0.6 39.6 %shard_map.59 = (f32[4,32,512]{2,1,0:T(8,128)S(1)}, f32[4,32,512]{2,1,0:T(8,128)S(1)}, f32[4,32,512]{2,1,0:T(8,128)S(1)}, f32[4,32,512]{2,1,0:T(8,128)S(1)}, f32...) custom-call(f32[4,32,512]{2,1,0:T(8,128)} %b_hbm.1, f32[4,32,512]{2,1,0:T(8,128)} %p_hbm.1, f32[4,32,512]{2,1,0:T(8,128)} %e_hbm.1, ...), custom_call_target="tpu_custom_call" | custom-call | tf_op jit(solution)/shard_map/pallas_call | solution.py:444
  40.3 0.9 %shard_map.60 = (f32[4,32,512]{2,1,0:T(8,128)}, f32[4,32,512]{2,1,0:T(8,128)}) custom-call(f32[4,32,512]{2,1,0:T(8,128)S(1)} %get-tuple-element.8.B, f32[4,32,512]{2,1,0:T(8,128)S(1)} %get-tuple-element.9.Z, f32[4,32,512]{2,1,0:T(8,128)S(1)} %get-tuple-element.10.U, f32[4,32,512]{2,1,0:T(8,128)S(1)} %get-tuple-element.11.Q, ...), custom_call_target="tpu_custom_call" | custom-call | tf_op jit(solution)/shard_map/pallas_call | solution.py:452

commit v5 on v4

--- a/solution.py
+++ b/solution.py
@@ -153,6 +153,8 @@
     for n, dev in enumerate(near):
         pl.when(earlier[n])(functools.partial(signal, close.at[mirror[n]], dev))
 
+    group_signals((here.at[0], here.at[1]), False)
+
     loads[0].wait()
     for p in range(planes):
         for j in range(tiles):
@@ -187,7 +189,6 @@
             YS[k, n] = ref[:, rends[k], :]
             YS[k, 3 + n] = ref[:, rseconds[k], :]
 
-    group_signals((here.at[0], here.at[1]), False)
     plan = [[] for _ in near]
     for k in range(2):
         plan[2 + k].append((YS.at[k], YB.at[1 - k]))

time: 41.3 us -> 41.4 us (level)
  no operation moved by 1% of the time
where the time goes in v5:
time: 41.4 us; the launch traced here: 41.2 us
  Pallas kernels  40.6 us (98%)
  between operations  0.64 us (2%)
    pallas_call x1, Pallas kernels, local(): pl.pallas_call(functools.partial(kernel, sizes), out_shape=(whole,) * 5 +...  39.7 us
    pallas_call x1, Pallas kernels, local(): pl.pallas_call(finish, out_shape=(whole, whole), in_specs=[vmem] * 6, out...  0.9 us

profile of v5, /device:TPU:1, one launch (start us, length us, event | category | flops | bytes accessed | tf_op | source)
XLA Modules:
  0.0 41.2 jit_solution(196881795523183043)
XLA Ops:
  0.6 39.7 %shard_map.59 = (f32[4,32,512]{2,1,0:T(8,128)S(1)}, f32[4,32,512]{2,1,0:T(8,128)S(1)}, f32[4,32,512]{2,1,0:T(8,128)S(1)}, f32[4,32,512]{2,1,0:T(8,128)S(1)}, f32...) custom-call(f32[4,32,512]{2,1,0:T(8,128)} %b_hbm.1, f32[4,32,512]{2,1,0:T(8,128)} %p_hbm.1, f32[4,32,512]{2,1,0:T(8,128)} %e_hbm.1, ...), custom_call_target="tpu_custom_call" | custom-call | tf_op jit(solution)/shard_map/pallas_call | solution.py:445
  40.3 0.9 %shard_map.60 = (f32[4,32,512]{2,1,0:T(8,128)}, f32[4,32,512]{2,1,0:T(8,128)}) custom-call(f32[4,32,512]{2,1,0:T(8,128)S(1)} %get-tuple-element.8.B, f32[4,32,512]{2,1,0:T(8,128)S(1)} %get-tuple-element.9.Z, f32[4,32,512]{2,1,0:T(8,128)S(1)} %get-tuple-element.10.U, f32[4,32,512]{2,1,0:T(8,128)S(1)} %get-tuple-element.11.Q, ...), custom_call_target="tpu_custom_call" | custom-call | tf_op jit(solution)/shard_map/pallas_call | solution.py:453
